TPU v7x, 256 devices: a whole 4x4x8 slice. The times are simulated.
256 devices in a mesh: src: 16 (over x_lo, y, core), tgt: 16 (over x_hi, z).
Axes of the slice: x: 4 (x_hi: 2, x_lo: 2; x = x_hi * 2 + x_lo), y: 4, z: 8, core: 2. Of those that a mesh axis runs over, the one named last changes fastest.
Arguments:
- src_coords: float32 [3, 98304], P(None, 'src'), may hold values from 0 to 1, as said below
- tgt_coords: float32 [3, 98304], P(None, 'tgt'), may hold values from 0 to 1
- src_scaling: float32 [32, 98304], P('tgt', 'src'), may hold values from 0.25 to 4
- src_mass: float32 [32, 98304], P('tgt', 'src'), may hold values from 0.25 to 4
- tgt_mass: float32 [32, 98304], P(None, 'tgt'), may hold values from 0.25 to 4
Outputs:
- new_src_scaling: float32 [32, 98304], P('tgt', 'src')
- tgt_scaling: float32 [32, 98304], P('src', 'tgt')
Inputs may be any that keep to these rules, and one draw needn't show every extreme that they name: `src_coords`: source points lie in the unit cube.
All inputs are finite; a program needn't handle non-finite values.
Results may differ from a plain program's by a relative error of at most 0.00036.
Values may be sent and summed in bfloat16 or wider, within the bound.
A program may use at most 64 MiB of HBM per device.

v0:
```python
import jax
import jax.numpy as jnp
from jax import lax
from jax.sharding import PartitionSpec as P


def kernel_block(xb, yt):
    dist = (xb[0][:, None] - yt[0][None, :]) ** 2
    dist = dist + (xb[1][:, None] - yt[1][None, :]) ** 2
    dist = dist + (xb[2][:, None] - yt[2][None, :]) ** 2
    return (180.0 * jnp.exp(-100.0 * dist)).astype(jnp.bfloat16)


def on_device(src_coords, tgt_coords, src_scaling, src_mass, tgt_mass):
    src_pts = src_coords.shape[1]
    tgt_pts = tgt_coords.shape[1]
    weights = tgt_mass.shape[0]
    block = min(512, src_pts)
    count = src_pts // block
    xs_blocks = src_coords.reshape(3, count, block).transpose(1, 0, 2)
    src_low = lax.all_gather(src_scaling.astype(jnp.bfloat16), "tgt", axis=0, tiled=True)
    u_blocks = src_low.reshape(weights, count, block).transpose(1, 0, 2)

    def col_step(carry, items):
        xb, ub = items
        kern = kernel_block(xb, tgt_coords)
        return (carry + jnp.dot(ub, kern, preferred_element_type=jnp.float32), None)

    col_terms, _ = lax.scan(
        col_step, jnp.zeros((weights, tgt_pts), jnp.float32), (xs_blocks, u_blocks)
    )
    total_src = src_pts * lax.axis_size("src")
    share_rows = weights // lax.axis_size("src")
    col_part = lax.psum_scatter(col_terms, "src", scatter_dimension=0, tiled=True)
    mass_part = lax.dynamic_slice_in_dim(
        tgt_mass, lax.axis_index("src") * share_rows, share_rows, 0
    )
    tgt_scaling = mass_part / (col_part / total_src)
    tgt_low = lax.all_gather(tgt_scaling.astype(jnp.bfloat16), "src", axis=0, tiled=True)

    def row_step(xb):
        kern = kernel_block(xb, tgt_coords)
        return jnp.dot(tgt_low, kern.T, preferred_element_type=jnp.float32)

    rows = lax.map(row_step, xs_blocks)
    row_terms = rows.transpose(1, 0, 2).reshape(weights, src_pts)
    row_part = lax.psum_scatter(row_terms, "tgt", scatter_dimension=0, tiled=True)
    total_tgt = tgt_pts * lax.axis_size("tgt")
    new_src_scaling = src_mass / (row_part / total_tgt)
    return (new_src_scaling, tgt_scaling)


def solution(mesh):
    placed = (P(None, "src"), P(None, "tgt"), P("tgt", "src"), P("tgt", "src"), P(None, "tgt"))
    return jax.shard_map(
        on_device,
        mesh=mesh,
        in_specs=placed,
        out_specs=(P("tgt", "src"), P("src", "tgt")),
        check_vma=False,
    )
```

profile of v0, /device:TPU:8, one launch (start us, length us, event | category | flops | bytes accessed | tf_op | source)
XLA Modules:
  0.0 511.5 jit_solution(1430984514631784748)
XLA Ops:
  7.2 0.8 convert_bitcast_fusion.1
  8.0 46.1 %all-gather = bf16[16,2,6144]{2,1,0:T(2,128)(2,1)S(1)} all-gather(bf16[1,2,6144]{2,1,0:T(2,128)(2,1)S(1)} %convert_bitcast_fusion.1), channel_id=1, replica_groups=mesh['src'=16,'tgt'=16] {'tgt'}, dimensions={0}, use_global_device_ids=true | all-gather | bytes 417792 | tf_op jit(solution)/shard_map/all_gather | solution.py:21
  54.2 0.2 reshape.32
  54.6 0.4 copy-done
  55.1 77.2 %while.22 = (s32[]{:T(128)}, f32[32,6144]{1,0:T(8,128)S(1)}, bf16[12,32,512]{2,1,0:T(8,128)(2,1)S(1)}, f32[12,3,512]{2,1,0:T(4,128)}, f32[3,6144]{1,0:T(4,128)S(1)}, /*index=5*/s32[]{:T(128)}, s32[]{:T(128)}, s32[]{}, s32[]{}) while((s32[]{:T(128)}, f32[32,6144]{1,0:T(8,128)S(1)}, bf16[12,32,512]{2,1,0:T(8,128)(2,1)S(1)}, ...), condition=%wide.region_1.2_spmd.clone, body=%wide.region_0.1_spmd.clone.sunk | while | flops 236322816 | bytes 1845391 | solution.py:29
  55.1 0.8 constant_dynamic-slice_fusion.9
  55.9 5.5 %convolution_add_fusion.2 = f32[32,6144]{1,0:T(8,128)S(1)} fusion(f32[6144]{0:T(1024)S(1)} %bitcast.69, f32[512]{0:T(512)S(1)} %bitcast.76, f32[6144]{0:T(1024)S(1)} %bitcast.70, f32[512]{0:T(512)S(1)} %bitcast.75, f32[6144]{0:T(1024)S(1)} %bitcast.68, f32[512]{0:T(512)S(1)} %bitcast.74, f32[32,6144]{1,0:T(8,128)S(1)} %get-tuple-element.216, ...), kind=kOutput, calls=%fused_computation.10.clone.1 | convolution fusion | flops 236322816 | bytes 1685509 | tf_op jit(solution)/shard_map/while/body/eval_jaxpr/dot_general | solution.py:27
  61.5 0.8 constant_dynamic-slice_fusion.9
  62.4 5.5 %convolution_add_fusion.2 = f32[32,6144]{1,0:T(8,128)S(1)} fusion(f32[6144]{0:T(1024)S(1)} %bitcast.69, f32[512]{0:T(512)S(1)} %bitcast.76, f32[6144]{0:T(1024)S(1)} %bitcast.70, f32[512]{0:T(512)S(1)} %bitcast.75, f32[6144]{0:T(1024)S(1)} %bitcast.68, f32[512]{0:T(512)S(1)} %bitcast.74, f32[32,6144]{1,0:T(8,128)S(1)} %get-tuple-element.216, ...), kind=kOutput, calls=%fused_computation.10.clone.1 | convolution fusion | flops 236322816 | bytes 1685509 | tf_op jit(solution)/shard_map/while/body/eval_jaxpr/dot_general | solution.py:27
  67.9 0.8 constant_dynamic-slice_fusion.9
  68.8 5.5 %convolution_add_fusion.2 = f32[32,6144]{1,0:T(8,128)S(1)} fusion(f32[6144]{0:T(1024)S(1)} %bitcast.69, f32[512]{0:T(512)S(1)} %bitcast.76, f32[6144]{0:T(1024)S(1)} %bitcast.70, f32[512]{0:T(512)S(1)} %bitcast.75, f32[6144]{0:T(1024)S(1)} %bitcast.68, f32[512]{0:T(512)S(1)} %bitcast.74, f32[32,6144]{1,0:T(8,128)S(1)} %get-tuple-element.216, ...), kind=kOutput, calls=%fused_computation.10.clone.1 | convolution fusion | flops 236322816 | bytes 1685509 | tf_op jit(solution)/shard_map/while/body/eval_jaxpr/dot_general | solution.py:27
  74.4 0.8 constant_dynamic-slice_fusion.9
  75.2 5.5 %convolution_add_fusion.2 = f32[32,6144]{1,0:T(8,128)S(1)} fusion(f32[6144]{0:T(1024)S(1)} %bitcast.69, f32[512]{0:T(512)S(1)} %bitcast.76, f32[6144]{0:T(1024)S(1)} %bitcast.70, f32[512]{0:T(512)S(1)} %bitcast.75, f32[6144]{0:T(1024)S(1)} %bitcast.68, f32[512]{0:T(512)S(1)} %bitcast.74, f32[32,6144]{1,0:T(8,128)S(1)} %get-tuple-element.216, ...), kind=kOutput, calls=%fused_computation.10.clone.1 | convolution fusion | flops 236322816 | bytes 1685509 | tf_op jit(solution)/shard_map/while/body/eval_jaxpr/dot_general | solution.py:27
  80.8 0.8 constant_dynamic-slice_fusion.9
  81.7 5.5 %convolution_add_fusion.2 = f32[32,6144]{1,0:T(8,128)S(1)} fusion(f32[6144]{0:T(1024)S(1)} %bitcast.69, f32[512]{0:T(512)S(1)} %bitcast.76, f32[6144]{0:T(1024)S(1)} %bitcast.70, f32[512]{0:T(512)S(1)} %bitcast.75, f32[6144]{0:T(1024)S(1)} %bitcast.68, f32[512]{0:T(512)S(1)} %bitcast.74, f32[32,6144]{1,0:T(8,128)S(1)} %get-tuple-element.216, ...), kind=kOutput, calls=%fused_computation.10.clone.1 | convolution fusion | flops 236322816 | bytes 1685509 | tf_op jit(solution)/shard_map/while/body/eval_jaxpr/dot_general | solution.py:27
  87.2 0.8 constant_dynamic-slice_fusion.9
  88.1 5.5 %convolution_add_fusion.2 = f32[32,6144]{1,0:T(8,128)S(1)} fusion(f32[6144]{0:T(1024)S(1)} %bitcast.69, f32[512]{0:T(512)S(1)} %bitcast.76, f32[6144]{0:T(1024)S(1)} %bitcast.70, f32[512]{0:T(512)S(1)} %bitcast.75, f32[6144]{0:T(1024)S(1)} %bitcast.68, f32[512]{0:T(512)S(1)} %bitcast.74, f32[32,6144]{1,0:T(8,128)S(1)} %get-tuple-element.216, ...), kind=kOutput, calls=%fused_computation.10.clone.1 | convolution fusion | flops 236322816 | bytes 1685509 | tf_op jit(solution)/shard_map/while/body/eval_jaxpr/dot_general | solution.py:27
  93.7 0.8 constant_dynamic-slice_fusion.9
  94.5 5.5 %convolution_add_fusion.2 = f32[32,6144]{1,0:T(8,128)S(1)} fusion(f32[6144]{0:T(1024)S(1)} %bitcast.69, f32[512]{0:T(512)S(1)} %bitcast.76, f32[6144]{0:T(1024)S(1)} %bitcast.70, f32[512]{0:T(512)S(1)} %bitcast.75, f32[6144]{0:T(1024)S(1)} %bitcast.68, f32[512]{0:T(512)S(1)} %bitcast.74, f32[32,6144]{1,0:T(8,128)S(1)} %get-tuple-element.216, ...), kind=kOutput, calls=%fused_computation.10.clone.1 | convolution fusion | flops 236322816 | bytes 1685509 | tf_op jit(solution)/shard_map/while/body/eval_jaxpr/dot_general | solution.py:27
  100.1 0.8 constant_dynamic-slice_fusion.9
  101.0 5.5 %convolution_add_fusion.2 = f32[32,6144]{1,0:T(8,128)S(1)} fusion(f32[6144]{0:T(1024)S(1)} %bitcast.69, f32[512]{0:T(512)S(1)} %bitcast.76, f32[6144]{0:T(1024)S(1)} %bitcast.70, f32[512]{0:T(512)S(1)} %bitcast.75, f32[6144]{0:T(1024)S(1)} %bitcast.68, f32[512]{0:T(512)S(1)} %bitcast.74, f32[32,6144]{1,0:T(8,128)S(1)} %get-tuple-element.216, ...), kind=kOutput, calls=%fused_computation.10.clone.1 | convolution fusion | flops 236322816 | bytes 1685509 | tf_op jit(solution)/shard_map/while/body/eval_jaxpr/dot_general | solution.py:27
  106.5 0.8 constant_dynamic-slice_fusion.9
  107.4 5.5 %convolution_add_fusion.2 = f32[32,6144]{1,0:T(8,128)S(1)} fusion(f32[6144]{0:T(1024)S(1)} %bitcast.69, f32[512]{0:T(512)S(1)} %bitcast.76, f32[6144]{0:T(1024)S(1)} %bitcast.70, f32[512]{0:T(512)S(1)} %bitcast.75, f32[6144]{0:T(1024)S(1)} %bitcast.68, f32[512]{0:T(512)S(1)} %bitcast.74, f32[32,6144]{1,0:T(8,128)S(1)} %get-tuple-element.216, ...), kind=kOutput, calls=%fused_computation.10.clone.1 | convolution fusion | flops 236322816 | bytes 1685509 | tf_op jit(solution)/shard_map/while/body/eval_jaxpr/dot_general | solution.py:27
  113.0 0.8 constant_dynamic-slice_fusion.9
  113.8 5.5 %convolution_add_fusion.2 = f32[32,6144]{1,0:T(8,128)S(1)} fusion(f32[6144]{0:T(1024)S(1)} %bitcast.69, f32[512]{0:T(512)S(1)} %bitcast.76, f32[6144]{0:T(1024)S(1)} %bitcast.70, f32[512]{0:T(512)S(1)} %bitcast.75, f32[6144]{0:T(1024)S(1)} %bitcast.68, f32[512]{0:T(512)S(1)} %bitcast.74, f32[32,6144]{1,0:T(8,128)S(1)} %get-tuple-element.216, ...), kind=kOutput, calls=%fused_computation.10.clone.1 | convolution fusion | flops 236322816 | bytes 1685509 | tf_op jit(solution)/shard_map/while/body/eval_jaxpr/dot_general | solution.py:27
  119.4 0.8 constant_dynamic-slice_fusion.9
  120.3 5.5 %convolution_add_fusion.2 = f32[32,6144]{1,0:T(8,128)S(1)} fusion(f32[6144]{0:T(1024)S(1)} %bitcast.69, f32[512]{0:T(512)S(1)} %bitcast.76, f32[6144]{0:T(1024)S(1)} %bitcast.70, f32[512]{0:T(512)S(1)} %bitcast.75, f32[6144]{0:T(1024)S(1)} %bitcast.68, f32[512]{0:T(512)S(1)} %bitcast.74, f32[32,6144]{1,0:T(8,128)S(1)} %get-tuple-element.216, ...), kind=kOutput, calls=%fused_computation.10.clone.1 | convolution fusion | flops 236322816 | bytes 1685509 | tf_op jit(solution)/shard_map/while/body/eval_jaxpr/dot_general | solution.py:27
  125.8 0.8 constant_dynamic-slice_fusion.9
  126.7 5.5 %convolution_add_fusion.2 = f32[32,6144]{1,0:T(8,128)S(1)} fusion(f32[6144]{0:T(1024)S(1)} %bitcast.69, f32[512]{0:T(512)S(1)} %bitcast.76, f32[6144]{0:T(1024)S(1)} %bitcast.70, f32[512]{0:T(512)S(1)} %bitcast.75, f32[6144]{0:T(1024)S(1)} %bitcast.68, f32[512]{0:T(512)S(1)} %bitcast.74, f32[32,6144]{1,0:T(8,128)S(1)} %get-tuple-element.216, ...), kind=kOutput, calls=%fused_computation.10.clone.1 | convolution fusion | flops 236322816 | bytes 1685509 | tf_op jit(solution)/shard_map/while/body/eval_jaxpr/dot_general | solution.py:27
  132.3 0.9 copy-done.1
  133.3 0.6 dynamic-slice
  134.5 113.5 %all-reduce.5.cloned.1.call-done = f32[32,6144]{1,0:T(8,128)} async-done(((f32[32,6144]{1,0:T(8,128)}), f32[32,6144]{1,0:T(8,128)}) %all-reduce.5.cloned.1.call-update) | async-done | bytes 786448
  248.0 1.7 convert_bitcast_fusion
  249.7 21.0 %all-gather.1 = bf16[16,2,6144]{2,1,0:T(2,128)(2,1)S(1)} all-gather(bf16[1,2,6144]{2,1,0:T(2,128)(2,1)S(1)} %get-tuple-element.106), channel_id=1, replica_groups=mesh['src'=16,'tgt'=16] {'src'}, dimensions={0}, use_global_device_ids=true | all-gather | bytes 417792 | tf_op jit(solution)/shard_map/all_gather | solution.py:39
  270.8 74.0 %while.21 = (s32[]{:T(128)}, f32[12,32,512]{2,1,0:T(8,128)S(1)}, f32[12,3,512]{2,1,0:T(4,128)}, f32[3,6144]{1,0:T(4,128)S(1)}, bf16[32,6144]{1,0:T(8,128)(2,1)S(1)}, /*index=5*/s32[]{:T(128)}, s32[]{:T(128)}, s32[]{}, s32[]{}) while((s32[]{:T(128)}, f32[12,32,512]{2,1,0:T(8,128)S(1)}, f32[12,3,512]{2,1,0:T(4,128)}, f32[3,6144]{1,0:T(4,128)S(1)}, ...), condition=%wide.region_4.5_spmd, body=%wide.region_3.4_spmd.sunk | while | flops 235929600 | bytes 698501 | solution.py:45
  270.8 0.8 constant_dynamic-slice_fusion.8
  271.7 5.3 %fusion.30 = f32[12,32,512]{2,1,0:T(8,128)S(1)} fusion(f32[12,32,512]{2,1,0:T(8,128)S(1)} %get-tuple-element.243, s32[]{:T(128)} %get-tuple-element.242, bf16[32,6144]{1,0:T(8,128)(2,1)S(1)} %get-tuple-element.255, f32[6144]{0:T(1024)S(1)} %bitcast.72, f32[512]{0:T(512)S(1)} %bitcast.79, f32[6144]{0:T(1024)S(1)} %bitcast.73, f32[512]{0:T(512)S(1)} %bitcast.78, ...), kind=kOutput, calls=%fused_computation.3.clone.1 | convolution fusion | flops 235929600 | bytes 538628 | tf_op jit(solution)/shard_map/while/body/eval_jaxpr/dot_general | solution.py:43
  277.0 0.8 constant_dynamic-slice_fusion.8
  277.9 5.3 %fusion.30 = f32[12,32,512]{2,1,0:T(8,128)S(1)} fusion(f32[12,32,512]{2,1,0:T(8,128)S(1)} %get-tuple-element.243, s32[]{:T(128)} %get-tuple-element.242, bf16[32,6144]{1,0:T(8,128)(2,1)S(1)} %get-tuple-element.255, f32[6144]{0:T(1024)S(1)} %bitcast.72, f32[512]{0:T(512)S(1)} %bitcast.79, f32[6144]{0:T(1024)S(1)} %bitcast.73, f32[512]{0:T(512)S(1)} %bitcast.78, ...), kind=kOutput, calls=%fused_computation.3.clone.1 | convolution fusion | flops 235929600 | bytes 538628 | tf_op jit(solution)/shard_map/while/body/eval_jaxpr/dot_general | solution.py:43
  283.2 0.8 constant_dynamic-slice_fusion.8
  284.1 5.3 %fusion.30 = f32[12,32,512]{2,1,0:T(8,128)S(1)} fusion(f32[12,32,512]{2,1,0:T(8,128)S(1)} %get-tuple-element.243, s32[]{:T(128)} %get-tuple-element.242, bf16[32,6144]{1,0:T(8,128)(2,1)S(1)} %get-tuple-element.255, f32[6144]{0:T(1024)S(1)} %bitcast.72, f32[512]{0:T(512)S(1)} %bitcast.79, f32[6144]{0:T(1024)S(1)} %bitcast.73, f32[512]{0:T(512)S(1)} %bitcast.78, ...), kind=kOutput, calls=%fused_computation.3.clone.1 | convolution fusion | flops 235929600 | bytes 538628 | tf_op jit(solution)/shard_map/while/body/eval_jaxpr/dot_general | solution.py:43
  289.3 0.8 constant_dynamic-slice_fusion.8
  290.2 5.3 %fusion.30 = f32[12,32,512]{2,1,0:T(8,128)S(1)} fusion(f32[12,32,512]{2,1,0:T(8,128)S(1)} %get-tuple-element.243, s32[]{:T(128)} %get-tuple-element.242, bf16[32,6144]{1,0:T(8,128)(2,1)S(1)} %get-tuple-element.255, f32[6144]{0:T(1024)S(1)} %bitcast.72, f32[512]{0:T(512)S(1)} %bitcast.79, f32[6144]{0:T(1024)S(1)} %bitcast.73, f32[512]{0:T(512)S(1)} %bitcast.78, ...), kind=kOutput, calls=%fused_computation.3.clone.1 | convolution fusion | flops 235929600 | bytes 538628 | tf_op jit(solution)/shard_map/while/body/eval_jaxpr/dot_general | solution.py:43
  295.5 0.8 constant_dynamic-slice_fusion.8
  296.4 5.3 %fusion.30 = f32[12,32,512]{2,1,0:T(8,128)S(1)} fusion(f32[12,32,512]{2,1,0:T(8,128)S(1)} %get-tuple-element.243, s32[]{:T(128)} %get-tuple-element.242, bf16[32,6144]{1,0:T(8,128)(2,1)S(1)} %get-tuple-element.255, f32[6144]{0:T(1024)S(1)} %bitcast.72, f32[512]{0:T(512)S(1)} %bitcast.79, f32[6144]{0:T(1024)S(1)} %bitcast.73, f32[512]{0:T(512)S(1)} %bitcast.78, ...), kind=kOutput, calls=%fused_computation.3.clone.1 | convolution fusion | flops 235929600 | bytes 538628 | tf_op jit(solution)/shard_map/while/body/eval_jaxpr/dot_general | solution.py:43
  301.7 0.8 constant_dynamic-slice_fusion.8
  302.6 5.3 %fusion.30 = f32[12,32,512]{2,1,0:T(8,128)S(1)} fusion(f32[12,32,512]{2,1,0:T(8,128)S(1)} %get-tuple-element.243, s32[]{:T(128)} %get-tuple-element.242, bf16[32,6144]{1,0:T(8,128)(2,1)S(1)} %get-tuple-element.255, f32[6144]{0:T(1024)S(1)} %bitcast.72, f32[512]{0:T(512)S(1)} %bitcast.79, f32[6144]{0:T(1024)S(1)} %bitcast.73, f32[512]{0:T(512)S(1)} %bitcast.78, ...), kind=kOutput, calls=%fused_computation.3.clone.1 | convolution fusion | flops 235929600 | bytes 538628 | tf_op jit(solution)/shard_map/while/body/eval_jaxpr/dot_general | solution.py:43
  307.8 0.8 constant_dynamic-slice_fusion.8
  308.7 5.3 %fusion.30 = f32[12,32,512]{2,1,0:T(8,128)S(1)} fusion(f32[12,32,512]{2,1,0:T(8,128)S(1)} %get-tuple-element.243, s32[]{:T(128)} %get-tuple-element.242, bf16[32,6144]{1,0:T(8,128)(2,1)S(1)} %get-tuple-element.255, f32[6144]{0:T(1024)S(1)} %bitcast.72, f32[512]{0:T(512)S(1)} %bitcast.79, f32[6144]{0:T(1024)S(1)} %bitcast.73, f32[512]{0:T(512)S(1)} %bitcast.78, ...), kind=kOutput, calls=%fused_computation.3.clone.1 | convolution fusion | flops 235929600 | bytes 538628 | tf_op jit(solution)/shard_map/while/body/eval_jaxpr/dot_general | solution.py:43
  314.0 0.8 constant_dynamic-slice_fusion.8
  314.9 5.3 %fusion.30 = f32[12,32,512]{2,1,0:T(8,128)S(1)} fusion(f32[12,32,512]{2,1,0:T(8,128)S(1)} %get-tuple-element.243, s32[]{:T(128)} %get-tuple-element.242, bf16[32,6144]{1,0:T(8,128)(2,1)S(1)} %get-tuple-element.255, f32[6144]{0:T(1024)S(1)} %bitcast.72, f32[512]{0:T(512)S(1)} %bitcast.79, f32[6144]{0:T(1024)S(1)} %bitcast.73, f32[512]{0:T(512)S(1)} %bitcast.78, ...), kind=kOutput, calls=%fused_computation.3.clone.1 | convolution fusion | flops 235929600 | bytes 538628 | tf_op jit(solution)/shard_map/while/body/eval_jaxpr/dot_general | solution.py:43
  320.2 0.8 constant_dynamic-slice_fusion.8
  321.1 5.3 %fusion.30 = f32[12,32,512]{2,1,0:T(8,128)S(1)} fusion(f32[12,32,512]{2,1,0:T(8,128)S(1)} %get-tuple-element.243, s32[]{:T(128)} %get-tuple-element.242, bf16[32,6144]{1,0:T(8,128)(2,1)S(1)} %get-tuple-element.255, f32[6144]{0:T(1024)S(1)} %bitcast.72, f32[512]{0:T(512)S(1)} %bitcast.79, f32[6144]{0:T(1024)S(1)} %bitcast.73, f32[512]{0:T(512)S(1)} %bitcast.78, ...), kind=kOutput, calls=%fused_computation.3.clone.1 | convolution fusion | flops 235929600 | bytes 538628 | tf_op jit(solution)/shard_map/while/body/eval_jaxpr/dot_general | solution.py:43
  326.3 0.8 constant_dynamic-slice_fusion.8
  327.2 5.3 %fusion.30 = f32[12,32,512]{2,1,0:T(8,128)S(1)} fusion(f32[12,32,512]{2,1,0:T(8,128)S(1)} %get-tuple-element.243, s32[]{:T(128)} %get-tuple-element.242, bf16[32,6144]{1,0:T(8,128)(2,1)S(1)} %get-tuple-element.255, f32[6144]{0:T(1024)S(1)} %bitcast.72, f32[512]{0:T(512)S(1)} %bitcast.79, f32[6144]{0:T(1024)S(1)} %bitcast.73, f32[512]{0:T(512)S(1)} %bitcast.78, ...), kind=kOutput, calls=%fused_computation.3.clone.1 | convolution fusion | flops 235929600 | bytes 538628 | tf_op jit(solution)/shard_map/while/body/eval_jaxpr/dot_general | solution.py:43
  332.5 0.8 constant_dynamic-slice_fusion.8
  333.4 5.3 %fusion.30 = f32[12,32,512]{2,1,0:T(8,128)S(1)} fusion(f32[12,32,512]{2,1,0:T(8,128)S(1)} %get-tuple-element.243, s32[]{:T(128)} %get-tuple-element.242, bf16[32,6144]{1,0:T(8,128)(2,1)S(1)} %get-tuple-element.255, f32[6144]{0:T(1024)S(1)} %bitcast.72, f32[512]{0:T(512)S(1)} %bitcast.79, f32[6144]{0:T(1024)S(1)} %bitcast.73, f32[512]{0:T(512)S(1)} %bitcast.78, ...), kind=kOutput, calls=%fused_computation.3.clone.1 | convolution fusion | flops 235929600 | bytes 538628 | tf_op jit(solution)/shard_map/while/body/eval_jaxpr/dot_general | solution.py:43
  338.7 0.8 constant_dynamic-slice_fusion.8
  339.6 5.3 %fusion.30 = f32[12,32,512]{2,1,0:T(8,128)S(1)} fusion(f32[12,32,512]{2,1,0:T(8,128)S(1)} %get-tuple-element.243, s32[]{:T(128)} %get-tuple-element.242, bf16[32,6144]{1,0:T(8,128)(2,1)S(1)} %get-tuple-element.255, f32[6144]{0:T(1024)S(1)} %bitcast.72, f32[512]{0:T(512)S(1)} %bitcast.79, f32[6144]{0:T(1024)S(1)} %bitcast.73, f32[512]{0:T(512)S(1)} %bitcast.78, ...), kind=kOutput, calls=%fused_computation.3.clone.1 | convolution fusion | flops 235929600 | bytes 538628 | tf_op jit(solution)/shard_map/while/body/eval_jaxpr/dot_general | solution.py:43
  344.8 1.0 copy.12
  345.8 0.7 copy-done.3
  346.5 0.6 dynamic-slice.2
  347.7 155.4 %all-reduce.7.cloned.1.call-done = f32[32,6144]{1,0:T(8,128)} async-done(((f32[32,6144]{1,0:T(8,128)}), f32[32,6144]{1,0:T(8,128)}) %all-reduce.7.cloned.1.call-update) | async-done | bytes 786448
  503.1 1.6 fusion.17
  (39 shorter events, 1.8 us)
Async XLA Ops:
  7.2 240.9 %all-reduce.5.cloned.1.call-start = ((), (), s32[]{:S(2)}) async-start(), calls=%async_computation | async-start | bytes 1572864
  54.2 0.9 copy-start
  132.3 0.9 copy-start.1
  132.3 1.0 copy-start.4
  133.2 369.9 %all-reduce.7.cloned.1.call-start = ((), (), s32[]{:S(2)}) async-start(), calls=%async_computation.1 | async-start | bytes 1572864
  345.8 0.7 copy-start.3
  345.8 157.3 %copy-start.2 = (f32[2,6144]{1,0:T(2,128)S(1)}, f32[2,6144]{1,0:T(2,128)}, u32[]{:S(2)}) copy-start(f32[2,6144]{1,0:T(2,128)} %param.12) | copy-start | bytes 147460
Sparse Core Ops, SparseCore 0:
  133.3 114.6 all-reduce.4
  346.0 157.0 all-reduce.6
where the time goes:
time: 513 us; the launch traced here: 512 us
  waiting for transfers between devices  269 us (52%)
  matrix products  130 us (25%)
  blocking collectives  67.1 us (13%)
  local copies, waits for them, and re-layouts  25.7 us (5%)
  between operations  15.4 us (3%)
    unnamed x4, waiting for transfers between devices  269 us
    dot_general x12, matrix products, col_step(): return (carry + jnp.dot(ub, kern, preferred_element_type=jnp.float32), None)  66.3 us
    dot_general x12, matrix products, row_step(): return jnp.dot(tgt_low, kern.T, preferred_element_type=jnp.float32)  63.4 us
    all_gather x1, blocking collectives, on_device(): lax.all_gather(src_scaling.astype(jnp.bfloat16), 'tgt', axis=0, tiled=True)  46.1 us
    slice x48, local copies, waits for them, and re-layouts, kernel_block(): dist = (xb[0][:, None] - yt[0][None, :]) ** 2  21 us
    all_gather x1, blocking collectives, on_device(): lax.all_gather(tgt_scaling.astype(jnp.bfloat16), 'src', axis=0, tiled=True)  21 us
  transfers between devices with their start and end apart: 2, of which 2 were waited for; matrix products, arithmetic and copies ran while one was open for 0% of the time, Pallas kernels for 0%

commit v1 on v0

--- a/solution.py
+++ b/solution.py
@@ -18,7 +18,12 @@
     block = min(512, src_pts)
     count = src_pts // block
     xs_blocks = src_coords.reshape(3, count, block).transpose(1, 0, 2)
-    src_low = lax.all_gather(src_scaling.astype(jnp.bfloat16), "tgt", axis=0, tiled=True)
+    src_low = jnp.concatenate(
+        lax.all_to_all(
+            jnp.stack([src_scaling.astype(jnp.bfloat16)] * lax.axis_size("tgt")), "tgt", 0, 0
+        ),
+        axis=0,
+    )
     u_blocks = src_low.reshape(weights, count, block).transpose(1, 0, 2)
 
     def col_step(carry, items):

time: 513 us -> 495 us (0.965)
  blocking collectives: 67.1 us -> 21 us
  waiting for transfers between devices: 269 us -> 285 us
  starting transfers between devices: 0.08 us -> 11.1 us
    all_gather x1 -> x0, blocking collectives: 46.1 us -> none  [on_device(): lax.all_gather(src_scaling.astype(jnp.bfloat16), 'tgt', axis=0, tiled=True)]
    all_to_all x0 -> x1, waiting for transfers between devices: none -> 14 us  [on_device(): lax.all_to_all(jnp.stack([src_scaling.astype(jnp.bfloat16)] * lax.axis_si...]
    all_to_all x0 -> x1, starting transfers between devices: none -> 11 us  [on_device(): lax.all_to_all(jnp.stack([src_scaling.astype(jnp.bfloat16)] * lax.axis_si...]
  transfers between devices with their start and end apart: 2 -> 3, of which waited for: 2 -> 3; matrix products, arithmetic and copies ran while one was open for 0% -> 0% of each run, Pallas kernels for 0% -> 0%
where the time goes in v1:
time: 495 us; the launch traced here: 493 us
  waiting for transfers between devices  285 us (58%)
  matrix products  130 us (26%)
  local copies, waits for them, and re-layouts  26.3 us (5%)
  blocking collectives  21 us (4%)
  between operations  15.5 us (3%)
  starting transfers between devices  11.1 us (2%)
    unnamed x4, waiting for transfers between devices  271 us
    dot_general x12, matrix products, col_step(): return (carry + jnp.dot(ub, kern, preferred_element_type=jnp.float32), None)  66.3 us
    dot_general x12, matrix products, row_step(): return jnp.dot(tgt_low, kern.T, preferred_element_type=jnp.float32)  63.4 us
    slice x48, local copies, waits for them, and re-layouts, kernel_block(): dist = (xb[0][:, None] - yt[0][None, :]) ** 2  21 us
    all_gather x1, blocking collectives, on_device(): lax.all_gather(tgt_scaling.astype(jnp.bfloat16), 'src', axis=0, tiled=True)  21 us
    all_to_all x1, waiting for transfers between devices, on_device(): lax.all_to_all(jnp.stack([src_scaling.astype(jnp.bfloat16)] * lax.axis_si...  14 us
    all_to_all x1, starting transfers between devices, on_device(): lax.all_to_all(jnp.stack([src_scaling.astype(jnp.bfloat16)] * lax.axis_si...  11 us
  transfers between devices with their start and end apart: 3, of which 3 were waited for; matrix products, arithmetic and copies ran while one was open for 0% of the time, Pallas kernels for 0%

profile of v1, /device:TPU:8, one launch (start us, length us, event | category | flops | bytes accessed | tf_op | source)
XLA Modules:
  0.0 493.4 jit_solution(17734462187348991447)
XLA Ops:
  7.2 0.8 convert_element_type.12
  8.0 0.9 stack.2
  8.9 11.0 %all-to-all-start = ((bf16[16,2,6144]{2,1,0:T(2,128)(2,1)}), bf16[16,2,6144]{2,1,0:T(2,128)(2,1)S(1)}, u32[]{:S(2)}, u32[]{:S(2)}) async-start(bf16[16,2,6144]{2,1,0:T(2,128)(2,1)} %stack.2), calls=%async_computation | async-start | bytes 786432 | tf_op jit(solution)/shard_map/all_to_all | solution.py:22
  20.0 14.0 %all-to-all-done = bf16[16,2,6144]{2,1,0:T(2,128)(2,1)S(1)} async-done(((bf16[16,2,6144]{2,1,0:T(2,128)(2,1)}), bf16[16,2,6144]{2,1,0:T(2,128)(2,1)S(1)}, u32[]{:S(2)}, u32[]{:S(2)}) %all-to-all-start) | async-done | bytes 393248 | tf_op jit(solution)/shard_map/all_to_all | solution.py:22
  34.6 77.2 %while.22 = (s32[]{:T(128)}, f32[32,6144]{1,0:T(8,128)S(1)}, bf16[12,32,512]{2,1,0:T(8,128)(2,1)S(1)}, f32[12,3,512]{2,1,0:T(4,128)}, f32[3,6144]{1,0:T(4,128)S(1)}, /*index=5*/s32[]{:T(128)}, s32[]{:T(128)}, s32[]{}, s32[]{}) while((s32[]{:T(128)}, f32[32,6144]{1,0:T(8,128)S(1)}, bf16[12,32,512]{2,1,0:T(8,128)(2,1)S(1)}, ...), condition=%wide.region_1.2_spmd.clone, body=%wide.region_0.1_spmd.clone.sunk | while | flops 236322816 | bytes 1845391 | solution.py:34
  34.6 0.8 constant_dynamic-slice_fusion.9
  35.5 5.5 %convolution_add_fusion.2 = f32[32,6144]{1,0:T(8,128)S(1)} fusion(f32[6144]{0:T(1024)S(1)} %bitcast.67, f32[512]{0:T(512)S(1)} %bitcast.74, f32[6144]{0:T(1024)S(1)} %bitcast.68, f32[512]{0:T(512)S(1)} %bitcast.73, f32[6144]{0:T(1024)S(1)} %bitcast.66, f32[512]{0:T(512)S(1)} %bitcast.72, f32[32,6144]{1,0:T(8,128)S(1)} %get-tuple-element.216, ...), kind=kOutput, calls=%fused_computation.10.clone.1 | convolution fusion | flops 236322816 | bytes 1685509 | tf_op jit(solution)/shard_map/while/body/eval_jaxpr/dot_general | solution.py:32
  41.0 0.8 constant_dynamic-slice_fusion.9
  41.9 5.5 %convolution_add_fusion.2 = f32[32,6144]{1,0:T(8,128)S(1)} fusion(f32[6144]{0:T(1024)S(1)} %bitcast.67, f32[512]{0:T(512)S(1)} %bitcast.74, f32[6144]{0:T(1024)S(1)} %bitcast.68, f32[512]{0:T(512)S(1)} %bitcast.73, f32[6144]{0:T(1024)S(1)} %bitcast.66, f32[512]{0:T(512)S(1)} %bitcast.72, f32[32,6144]{1,0:T(8,128)S(1)} %get-tuple-element.216, ...), kind=kOutput, calls=%fused_computation.10.clone.1 | convolution fusion | flops 236322816 | bytes 1685509 | tf_op jit(solution)/shard_map/while/body/eval_jaxpr/dot_general | solution.py:32
  47.5 0.8 constant_dynamic-slice_fusion.9
  48.3 5.5 %convolution_add_fusion.2 = f32[32,6144]{1,0:T(8,128)S(1)} fusion(f32[6144]{0:T(1024)S(1)} %bitcast.67, f32[512]{0:T(512)S(1)} %bitcast.74, f32[6144]{0:T(1024)S(1)} %bitcast.68, f32[512]{0:T(512)S(1)} %bitcast.73, f32[6144]{0:T(1024)S(1)} %bitcast.66, f32[512]{0:T(512)S(1)} %bitcast.72, f32[32,6144]{1,0:T(8,128)S(1)} %get-tuple-element.216, ...), kind=kOutput, calls=%fused_computation.10.clone.1 | convolution fusion | flops 236322816 | bytes 1685509 | tf_op jit(solution)/shard_map/while/body/eval_jaxpr/dot_general | solution.py:32
  53.9 0.8 constant_dynamic-slice_fusion.9
  54.8 5.5 %convolution_add_fusion.2 = f32[32,6144]{1,0:T(8,128)S(1)} fusion(f32[6144]{0:T(1024)S(1)} %bitcast.67, f32[512]{0:T(512)S(1)} %bitcast.74, f32[6144]{0:T(1024)S(1)} %bitcast.68, f32[512]{0:T(512)S(1)} %bitcast.73, f32[6144]{0:T(1024)S(1)} %bitcast.66, f32[512]{0:T(512)S(1)} %bitcast.72, f32[32,6144]{1,0:T(8,128)S(1)} %get-tuple-element.216, ...), kind=kOutput, calls=%fused_computation.10.clone.1 | convolution fusion | flops 236322816 | bytes 1685509 | tf_op jit(solution)/shard_map/while/body/eval_jaxpr/dot_general | solution.py:32
  60.3 0.8 constant_dynamic-slice_fusion.9
  61.2 5.5 %convolution_add_fusion.2 = f32[32,6144]{1,0:T(8,128)S(1)} fusion(f32[6144]{0:T(1024)S(1)} %bitcast.67, f32[512]{0:T(512)S(1)} %bitcast.74, f32[6144]{0:T(1024)S(1)} %bitcast.68, f32[512]{0:T(512)S(1)} %bitcast.73, f32[6144]{0:T(1024)S(1)} %bitcast.66, f32[512]{0:T(512)S(1)} %bitcast.72, f32[32,6144]{1,0:T(8,128)S(1)} %get-tuple-element.216, ...), kind=kOutput, calls=%fused_computation.10.clone.1 | convolution fusion | flops 236322816 | bytes 1685509 | tf_op jit(solution)/shard_map/while/body/eval_jaxpr/dot_general | solution.py:32
  66.8 0.8 constant_dynamic-slice_fusion.9
  67.6 5.5 %convolution_add_fusion.2 = f32[32,6144]{1,0:T(8,128)S(1)} fusion(f32[6144]{0:T(1024)S(1)} %bitcast.67, f32[512]{0:T(512)S(1)} %bitcast.74, f32[6144]{0:T(1024)S(1)} %bitcast.68, f32[512]{0:T(512)S(1)} %bitcast.73, f32[6144]{0:T(1024)S(1)} %bitcast.66, f32[512]{0:T(512)S(1)} %bitcast.72, f32[32,6144]{1,0:T(8,128)S(1)} %get-tuple-element.216, ...), kind=kOutput, calls=%fused_computation.10.clone.1 | convolution fusion | flops 236322816 | bytes 1685509 | tf_op jit(solution)/shard_map/while/body/eval_jaxpr/dot_general | solution.py:32
  73.2 0.8 constant_dynamic-slice_fusion.9
  74.1 5.5 %convolution_add_fusion.2 = f32[32,6144]{1,0:T(8,128)S(1)} fusion(f32[6144]{0:T(1024)S(1)} %bitcast.67, f32[512]{0:T(512)S(1)} %bitcast.74, f32[6144]{0:T(1024)S(1)} %bitcast.68, f32[512]{0:T(512)S(1)} %bitcast.73, f32[6144]{0:T(1024)S(1)} %bitcast.66, f32[512]{0:T(512)S(1)} %bitcast.72, f32[32,6144]{1,0:T(8,128)S(1)} %get-tuple-element.216, ...), kind=kOutput, calls=%fused_computation.10.clone.1 | convolution fusion | flops 236322816 | bytes 1685509 | tf_op jit(solution)/shard_map/while/body/eval_jaxpr/dot_general | solution.py:32
  79.6 0.8 constant_dynamic-slice_fusion.9
  80.5 5.5 %convolution_add_fusion.2 = f32[32,6144]{1,0:T(8,128)S(1)} fusion(f32[6144]{0:T(1024)S(1)} %bitcast.67, f32[512]{0:T(512)S(1)} %bitcast.74, f32[6144]{0:T(1024)S(1)} %bitcast.68, f32[512]{0:T(512)S(1)} %bitcast.73, f32[6144]{0:T(1024)S(1)} %bitcast.66, f32[512]{0:T(512)S(1)} %bitcast.72, f32[32,6144]{1,0:T(8,128)S(1)} %get-tuple-element.216, ...), kind=kOutput, calls=%fused_computation.10.clone.1 | convolution fusion | flops 236322816 | bytes 1685509 | tf_op jit(solution)/shard_map/while/body/eval_jaxpr/dot_general | solution.py:32
  86.1 0.8 constant_dynamic-slice_fusion.9
  86.9 5.5 %convolution_add_fusion.2 = f32[32,6144]{1,0:T(8,128)S(1)} fusion(f32[6144]{0:T(1024)S(1)} %bitcast.67, f32[512]{0:T(512)S(1)} %bitcast.74, f32[6144]{0:T(1024)S(1)} %bitcast.68, f32[512]{0:T(512)S(1)} %bitcast.73, f32[6144]{0:T(1024)S(1)} %bitcast.66, f32[512]{0:T(512)S(1)} %bitcast.72, f32[32,6144]{1,0:T(8,128)S(1)} %get-tuple-element.216, ...), kind=kOutput, calls=%fused_computation.10.clone.1 | convolution fusion | flops 236322816 | bytes 1685509 | tf_op jit(solution)/shard_map/while/body/eval_jaxpr/dot_general | solution.py:32
  92.5 0.8 constant_dynamic-slice_fusion.9
  93.4 5.5 %convolution_add_fusion.2 = f32[32,6144]{1,0:T(8,128)S(1)} fusion(f32[6144]{0:T(1024)S(1)} %bitcast.67, f32[512]{0:T(512)S(1)} %bitcast.74, f32[6144]{0:T(1024)S(1)} %bitcast.68, f32[512]{0:T(512)S(1)} %bitcast.73, f32[6144]{0:T(1024)S(1)} %bitcast.66, f32[512]{0:T(512)S(1)} %bitcast.72, f32[32,6144]{1,0:T(8,128)S(1)} %get-tuple-element.216, ...), kind=kOutput, calls=%fused_computation.10.clone.1 | convolution fusion | flops 236322816 | bytes 1685509 | tf_op jit(solution)/shard_map/while/body/eval_jaxpr/dot_general | solution.py:32
  98.9 0.8 constant_dynamic-slice_fusion.9
  99.8 5.5 %convolution_add_fusion.2 = f32[32,6144]{1,0:T(8,128)S(1)} fusion(f32[6144]{0:T(1024)S(1)} %bitcast.67, f32[512]{0:T(512)S(1)} %bitcast.74, f32[6144]{0:T(1024)S(1)} %bitcast.68, f32[512]{0:T(512)S(1)} %bitcast.73, f32[6144]{0:T(1024)S(1)} %bitcast.66, f32[512]{0:T(512)S(1)} %bitcast.72, f32[32,6144]{1,0:T(8,128)S(1)} %get-tuple-element.216, ...), kind=kOutput, calls=%fused_computation.10.clone.1 | convolution fusion | flops 236322816 | bytes 1685509 | tf_op jit(solution)/shard_map/while/body/eval_jaxpr/dot_general | solution.py:32
  105.4 0.8 constant_dynamic-slice_fusion.9
  106.2 5.5 %convolution_add_fusion.2 = f32[32,6144]{1,0:T(8,128)S(1)} fusion(f32[6144]{0:T(1024)S(1)} %bitcast.67, f32[512]{0:T(512)S(1)} %bitcast.74, f32[6144]{0:T(1024)S(1)} %bitcast.68, f32[512]{0:T(512)S(1)} %bitcast.73, f32[6144]{0:T(1024)S(1)} %bitcast.66, f32[512]{0:T(512)S(1)} %bitcast.72, f32[32,6144]{1,0:T(8,128)S(1)} %get-tuple-element.216, ...), kind=kOutput, calls=%fused_computation.10.clone.1 | convolution fusion | flops 236322816 | bytes 1685509 | tf_op jit(solution)/shard_map/while/body/eval_jaxpr/dot_general | solution.py:32
  111.8 0.9 copy-done.1
  112.8 0.6 dynamic-slice
  114.1 115.8 %all-reduce.5.cloned.1.call-done = f32[32,6144]{1,0:T(8,128)} async-done(((f32[32,6144]{1,0:T(8,128)}), f32[32,6144]{1,0:T(8,128)}) %all-reduce.5.cloned.1.call-update) | async-done | bytes 786448
  229.9 1.7 convert_bitcast_fusion
  231.6 21.0 %all-gather = bf16[16,2,6144]{2,1,0:T(2,128)(2,1)S(1)} all-gather(bf16[1,2,6144]{2,1,0:T(2,128)(2,1)S(1)} %get-tuple-element.106), channel_id=1, replica_groups=mesh['src'=16,'tgt'=16] {'src'}, dimensions={0}, use_global_device_ids=true | all-gather | bytes 417792 | tf_op jit(solution)/shard_map/all_gather | solution.py:44
  252.7 74.0 %while.21 = (s32[]{:T(128)}, f32[12,32,512]{2,1,0:T(8,128)S(1)}, f32[12,3,512]{2,1,0:T(4,128)}, f32[3,6144]{1,0:T(4,128)S(1)}, bf16[32,6144]{1,0:T(8,128)(2,1)S(1)}, /*index=5*/s32[]{:T(128)}, s32[]{:T(128)}, s32[]{}, s32[]{}) while((s32[]{:T(128)}, f32[12,32,512]{2,1,0:T(8,128)S(1)}, f32[12,3,512]{2,1,0:T(4,128)}, f32[3,6144]{1,0:T(4,128)S(1)}, ...), condition=%wide.region_4.5_spmd, body=%wide.region_3.4_spmd.sunk | while | flops 235929600 | bytes 698501 | solution.py:50
  252.7 0.8 constant_dynamic-slice_fusion.8
  253.6 5.3 %fusion.30 = f32[12,32,512]{2,1,0:T(8,128)S(1)} fusion(f32[12,32,512]{2,1,0:T(8,128)S(1)} %get-tuple-element.243, s32[]{:T(128)} %get-tuple-element.242, bf16[32,6144]{1,0:T(8,128)(2,1)S(1)} %get-tuple-element.255, f32[6144]{0:T(1024)S(1)} %bitcast.70, f32[512]{0:T(512)S(1)} %bitcast.77, f32[6144]{0:T(1024)S(1)} %bitcast.71, f32[512]{0:T(512)S(1)} %bitcast.76, ...), kind=kOutput, calls=%fused_computation.3.clone.1 | convolution fusion | flops 235929600 | bytes 538628 | tf_op jit(solution)/shard_map/while/body/eval_jaxpr/dot_general | solution.py:48
  258.9 0.8 constant_dynamic-slice_fusion.8
  259.8 5.3 %fusion.30 = f32[12,32,512]{2,1,0:T(8,128)S(1)} fusion(f32[12,32,512]{2,1,0:T(8,128)S(1)} %get-tuple-element.243, s32[]{:T(128)} %get-tuple-element.242, bf16[32,6144]{1,0:T(8,128)(2,1)S(1)} %get-tuple-element.255, f32[6144]{0:T(1024)S(1)} %bitcast.70, f32[512]{0:T(512)S(1)} %bitcast.77, f32[6144]{0:T(1024)S(1)} %bitcast.71, f32[512]{0:T(512)S(1)} %bitcast.76, ...), kind=kOutput, calls=%fused_computation.3.clone.1 | convolution fusion | flops 235929600 | bytes 538628 | tf_op jit(solution)/shard_map/while/body/eval_jaxpr/dot_general | solution.py:48
  265.0 0.8 constant_dynamic-slice_fusion.8
  265.9 5.3 %fusion.30 = f32[12,32,512]{2,1,0:T(8,128)S(1)} fusion(f32[12,32,512]{2,1,0:T(8,128)S(1)} %get-tuple-element.243, s32[]{:T(128)} %get-tuple-element.242, bf16[32,6144]{1,0:T(8,128)(2,1)S(1)} %get-tuple-element.255, f32[6144]{0:T(1024)S(1)} %bitcast.70, f32[512]{0:T(512)S(1)} %bitcast.77, f32[6144]{0:T(1024)S(1)} %bitcast.71, f32[512]{0:T(512)S(1)} %bitcast.76, ...), kind=kOutput, calls=%fused_computation.3.clone.1 | convolution fusion | flops 235929600 | bytes 538628 | tf_op jit(solution)/shard_map/while/body/eval_jaxpr/dot_general | solution.py:48
  271.2 0.8 constant_dynamic-slice_fusion.8
  272.1 5.3 %fusion.30 = f32[12,32,512]{2,1,0:T(8,128)S(1)} fusion(f32[12,32,512]{2,1,0:T(8,128)S(1)} %get-tuple-element.243, s32[]{:T(128)} %get-tuple-element.242, bf16[32,6144]{1,0:T(8,128)(2,1)S(1)} %get-tuple-element.255, f32[6144]{0:T(1024)S(1)} %bitcast.70, f32[512]{0:T(512)S(1)} %bitcast.77, f32[6144]{0:T(1024)S(1)} %bitcast.71, f32[512]{0:T(512)S(1)} %bitcast.76, ...), kind=kOutput, calls=%fused_computation.3.clone.1 | convolution fusion | flops 235929600 | bytes 538628 | tf_op jit(solution)/shard_map/while/body/eval_jaxpr/dot_general | solution.py:48
  277.4 0.8 constant_dynamic-slice_fusion.8
  278.3 5.3 %fusion.30 = f32[12,32,512]{2,1,0:T(8,128)S(1)} fusion(f32[12,32,512]{2,1,0:T(8,128)S(1)} %get-tuple-element.243, s32[]{:T(128)} %get-tuple-element.242, bf16[32,6144]{1,0:T(8,128)(2,1)S(1)} %get-tuple-element.255, f32[6144]{0:T(1024)S(1)} %bitcast.70, f32[512]{0:T(512)S(1)} %bitcast.77, f32[6144]{0:T(1024)S(1)} %bitcast.71, f32[512]{0:T(512)S(1)} %bitcast.76, ...), kind=kOutput, calls=%fused_computation.3.clone.1 | convolution fusion | flops 235929600 | bytes 538628 | tf_op jit(solution)/shard_map/while/body/eval_jaxpr/dot_general | solution.py:48
  283.5 0.8 constant_dynamic-slice_fusion.8
  284.4 5.3 %fusion.30 = f32[12,32,512]{2,1,0:T(8,128)S(1)} fusion(f32[12,32,512]{2,1,0:T(8,128)S(1)} %get-tuple-element.243, s32[]{:T(128)} %get-tuple-element.242, bf16[32,6144]{1,0:T(8,128)(2,1)S(1)} %get-tuple-element.255, f32[6144]{0:T(1024)S(1)} %bitcast.70, f32[512]{0:T(512)S(1)} %bitcast.77, f32[6144]{0:T(1024)S(1)} %bitcast.71, f32[512]{0:T(512)S(1)} %bitcast.76, ...), kind=kOutput, calls=%fused_computation.3.clone.1 | convolution fusion | flops 235929600 | bytes 538628 | tf_op jit(solution)/shard_map/while/body/eval_jaxpr/dot_general | solution.py:48
  289.7 0.8 constant_dynamic-slice_fusion.8
  290.6 5.3 %fusion.30 = f32[12,32,512]{2,1,0:T(8,128)S(1)} fusion(f32[12,32,512]{2,1,0:T(8,128)S(1)} %get-tuple-element.243, s32[]{:T(128)} %get-tuple-element.242, bf16[32,6144]{1,0:T(8,128)(2,1)S(1)} %get-tuple-element.255, f32[6144]{0:T(1024)S(1)} %bitcast.70, f32[512]{0:T(512)S(1)} %bitcast.77, f32[6144]{0:T(1024)S(1)} %bitcast.71, f32[512]{0:T(512)S(1)} %bitcast.76, ...), kind=kOutput, calls=%fused_computation.3.clone.1 | convolution fusion | flops 235929600 | bytes 538628 | tf_op jit(solution)/shard_map/while/body/eval_jaxpr/dot_general | solution.py:48
  295.9 0.8 constant_dynamic-slice_fusion.8
  296.8 5.3 %fusion.30 = f32[12,32,512]{2,1,0:T(8,128)S(1)} fusion(f32[12,32,512]{2,1,0:T(8,128)S(1)} %get-tuple-element.243, s32[]{:T(128)} %get-tuple-element.242, bf16[32,6144]{1,0:T(8,128)(2,1)S(1)} %get-tuple-element.255, f32[6144]{0:T(1024)S(1)} %bitcast.70, f32[512]{0:T(512)S(1)} %bitcast.77, f32[6144]{0:T(1024)S(1)} %bitcast.71, f32[512]{0:T(512)S(1)} %bitcast.76, ...), kind=kOutput, calls=%fused_computation.3.clone.1 | convolution fusion | flops 235929600 | bytes 538628 | tf_op jit(solution)/shard_map/while/body/eval_jaxpr/dot_general | solution.py:48
  302.0 0.8 constant_dynamic-slice_fusion.8
  302.9 5.3 %fusion.30 = f32[12,32,512]{2,1,0:T(8,128)S(1)} fusion(f32[12,32,512]{2,1,0:T(8,128)S(1)} %get-tuple-element.243, s32[]{:T(128)} %get-tuple-element.242, bf16[32,6144]{1,0:T(8,128)(2,1)S(1)} %get-tuple-element.255, f32[6144]{0:T(1024)S(1)} %bitcast.70, f32[512]{0:T(512)S(1)} %bitcast.77, f32[6144]{0:T(1024)S(1)} %bitcast.71, f32[512]{0:T(512)S(1)} %bitcast.76, ...), kind=kOutput, calls=%fused_computation.3.clone.1 | convolution fusion | flops 235929600 | bytes 538628 | tf_op jit(solution)/shard_map/while/body/eval_jaxpr/dot_general | solution.py:48
  308.2 0.8 constant_dynamic-slice_fusion.8
  309.1 5.3 %fusion.30 = f32[12,32,512]{2,1,0:T(8,128)S(1)} fusion(f32[12,32,512]{2,1,0:T(8,128)S(1)} %get-tuple-element.243, s32[]{:T(128)} %get-tuple-element.242, bf16[32,6144]{1,0:T(8,128)(2,1)S(1)} %get-tuple-element.255, f32[6144]{0:T(1024)S(1)} %bitcast.70, f32[512]{0:T(512)S(1)} %bitcast.77, f32[6144]{0:T(1024)S(1)} %bitcast.71, f32[512]{0:T(512)S(1)} %bitcast.76, ...), kind=kOutput, calls=%fused_computation.3.clone.1 | convolution fusion | flops 235929600 | bytes 538628 | tf_op jit(solution)/shard_map/while/body/eval_jaxpr/dot_general | solution.py:48
  314.4 0.8 constant_dynamic-slice_fusion.8
  315.3 5.3 %fusion.30 = f32[12,32,512]{2,1,0:T(8,128)S(1)} fusion(f32[12,32,512]{2,1,0:T(8,128)S(1)} %get-tuple-element.243, s32[]{:T(128)} %get-tuple-element.242, bf16[32,6144]{1,0:T(8,128)(2,1)S(1)} %get-tuple-element.255, f32[6144]{0:T(1024)S(1)} %bitcast.70, f32[512]{0:T(512)S(1)} %bitcast.77, f32[6144]{0:T(1024)S(1)} %bitcast.71, f32[512]{0:T(512)S(1)} %bitcast.76, ...), kind=kOutput, calls=%fused_computation.3.clone.1 | convolution fusion | flops 235929600 | bytes 538628 | tf_op jit(solution)/shard_map/while/body/eval_jaxpr/dot_general | solution.py:48
  320.5 0.8 constant_dynamic-slice_fusion.8
  321.4 5.3 %fusion.30 = f32[12,32,512]{2,1,0:T(8,128)S(1)} fusion(f32[12,32,512]{2,1,0:T(8,128)S(1)} %get-tuple-element.243, s32[]{:T(128)} %get-tuple-element.242, bf16[32,6144]{1,0:T(8,128)(2,1)S(1)} %get-tuple-element.255, f32[6144]{0:T(1024)S(1)} %bitcast.70, f32[512]{0:T(512)S(1)} %bitcast.77, f32[6144]{0:T(1024)S(1)} %bitcast.71, f32[512]{0:T(512)S(1)} %bitcast.76, ...), kind=kOutput, calls=%fused_computation.3.clone.1 | convolution fusion | flops 235929600 | bytes 538628 | tf_op jit(solution)/shard_map/while/body/eval_jaxpr/dot_general | solution.py:48
  326.7 1.0 copy.12
  327.7 0.7 copy-done.3
  328.4 0.6 dynamic-slice.2
  329.6 155.4 %all-reduce.7.cloned.1.call-done = f32[32,6144]{1,0:T(8,128)} async-done(((f32[32,6144]{1,0:T(8,128)}), f32[32,6144]{1,0:T(8,128)}) %all-reduce.7.cloned.1.call-update) | async-done | bytes 786448
  485.0 1.6 fusion.17
  (41 shorter events, 2.0 us)
Async XLA Ops:
  8.9 25.2 %all-to-all-start = ((bf16[16,2,6144]{2,1,0:T(2,128)(2,1)}), bf16[16,2,6144]{2,1,0:T(2,128)(2,1)S(1)}, u32[]{:S(2)}, u32[]{:S(2)}) async-start(bf16[16,2,6144]{2,1,0:T(2,128)(2,1)} %stack.2), calls=%async_computation | async-start | bytes 786432 | tf_op jit(solution)/shard_map/all_to_all | solution.py:22
  20.0 209.9 %all-reduce.5.cloned.1.call-start = ((), (), s32[]{:S(2)}) async-start(), calls=%async_computation.1 | async-start | bytes 1572864
  20.0 14.5 %copy-start = (f32[3,6144]{1,0:T(4,128)S(1)}, f32[3,6144]{1,0:T(4,128)}, u32[]{:S(2)}) copy-start(f32[3,6144]{1,0:T(4,128)} %param.10) | copy-start | bytes 221188
  111.8 0.9 copy-start.1
  111.8 1.0 copy-start.4
  112.7 372.3 %all-reduce.7.cloned.1.call-start = ((), (), s32[]{:S(2)}) async-start(), calls=%async_computation.2 | async-start | bytes 1572864
  327.7 0.7 copy-start.3
  327.7 157.3 %copy-start.2 = (f32[2,6144]{1,0:T(2,128)S(1)}, f32[2,6144]{1,0:T(2,128)}, u32[]{:S(2)}) copy-start(f32[2,6144]{1,0:T(2,128)} %param.12) | copy-start | bytes 147460
Sparse Core Ops, SparseCore 0:
  112.9 116.9 all-reduce.4
  327.9 157.0 all-reduce.6
